TPU v7x, 512 devices: a whole 4x8x8 slice. The times are simulated.
512 devices in a mesh: frames: 128 (over z, y, core), heads: 4 (over x).
Axes of the slice: x: 4, y: 8, z: 8, core: 2. Of those that a mesh axis runs over, the one named last changes fastest.
Arguments:
- activations: bfloat16 [16384, 2048], P('frames', 'heads'), may hold values from -6 to 6
- norm_gain: bfloat16 [2048], P('heads'), may hold values from 0.099609375 to 1.8984375
- w_query: bfloat16 [2048, 2048], P('frames', 'heads'), may hold values from -0.125 to 0.125
- w_key: bfloat16 [2048, 2048], P('frames', 'heads'), may hold values from -0.125 to 0.125
- w_value: bfloat16 [2048, 2048], P('frames', 'heads'), may hold values from -0.125 to 0.125
- out_grad: bfloat16 [16384, 2048], P('frames', 'heads'), may hold values from -6 to 6
Outputs:
- input_grad: bfloat16 [16384, 2048], P('frames', 'heads')
- gain_grad: float32 [2048], P('heads')
All inputs are finite; a program needn't handle non-finite values.
Results may differ from a plain program's by a relative error of at most 0.009.
Values may be sent and summed in bfloat16 or wider, within the bound.
A program may use at most 64 MiB of HBM per device.

v0:
```python
import jax
import jax.numpy as jnp
from jax import lax
from jax.sharding import PartitionSpec as P

D = 2048
HDIM = 128


EPS = 1e-05


def temporal_backward(pieces):
    queries, key_rows, value_rows, grad_rows = pieces
    frame_count, unit_dim, item_count, inner_width = queries.shape
    head_count = inner_width // HDIM
    form_shape = (frame_count, item_count, head_count, HDIM)
    queries = queries.reshape(form_shape)
    key_rows = key_rows.reshape(form_shape)
    value_rows = value_rows.reshape(form_shape)
    grad_rows = grad_rows.reshape(form_shape)
    score_scale = HDIM ** (-0.5)
    scores = (
        jnp.einsum("tnhd,unhd->nhtu", queries, key_rows, preferred_element_type=jnp.float32)
        * score_scale
    )
    later_idx = lax.broadcasted_iota(jnp.int32, (frame_count, frame_count), 0)
    earlier_idx = lax.broadcasted_iota(jnp.int32, (frame_count, frame_count), 1)
    causal = later_idx >= earlier_idx
    exp_scores = jnp.where(causal, jnp.exp(jnp.where(causal, scores, 0.0)), 0.0)
    weights = exp_scores / jnp.sum(exp_scores, axis=-1, keepdims=True)
    weights_low = weights.astype(jnp.bfloat16)
    dweights = jnp.einsum(
        "tnhd,unhd->nhtu", grad_rows, value_rows, preferred_element_type=jnp.float32
    )
    row_delta = jnp.sum(weights * dweights, axis=-1, keepdims=True)
    dscores = (weights * (dweights - row_delta) * score_scale).astype(jnp.bfloat16)
    dquery = jnp.einsum(
        "nhtu,unhd->tnhd", dscores, key_rows, preferred_element_type=jnp.float32
    ).astype(jnp.bfloat16)
    dkey = jnp.einsum(
        "nhtu,tnhd->unhd", dscores, queries, preferred_element_type=jnp.float32
    ).astype(jnp.bfloat16)
    dvalue = jnp.einsum(
        "nhtu,tnhd->unhd", weights_low, grad_rows, preferred_element_type=jnp.float32
    ).astype(jnp.bfloat16)
    flat_shape = (frame_count, unit_dim, item_count, inner_width)
    return (dquery.reshape(flat_shape), dkey.reshape(flat_shape), dvalue.reshape(flat_shape))


def shards(activations, norm_gain, w_query, w_key, w_value, out_grad):
    positions, width = activations.shape
    inner_width = w_query.shape[1]
    frame_devices = lax.axis_size("frames")
    values_f = activations.astype(jnp.float32)
    gain_f = norm_gain.astype(jnp.float32)
    square_sum = lax.psum(jnp.sum(values_f * values_f, axis=1), "heads")
    inverse_rms = lax.rsqrt(square_sum / D + EPS)[:, None]
    normed_own = (values_f * inverse_rms * gain_f).astype(jnp.bfloat16)
    normed = lax.all_gather(normed_own, "heads", axis=1, tiled=True)
    projected = jnp.dot(
        normed,
        jnp.concatenate(
            (
                lax.all_gather(w_query, "frames", axis=0, tiled=True),
                lax.all_gather(w_key, "frames", axis=0, tiled=True),
                lax.all_gather(w_value, "frames", axis=0, tiled=True),
            ),
            axis=1,
        ),
        preferred_element_type=jnp.float32,
    )
    mixed = projected.astype(jnp.bfloat16)
    split_shape = (1, frame_devices, positions // frame_devices, inner_width)
    queries = mixed[:, :inner_width].reshape(split_shape)
    key_rows = mixed[:, inner_width : 2 * inner_width].reshape(split_shape)
    value_rows = mixed[:, 2 * inner_width :].reshape(split_shape)
    grad_split = out_grad.reshape(split_shape)
    layout = (queries, key_rows, value_rows, grad_split)
    dquery, dkey, dvalue = temporal_backward(
        (
            lax.all_to_all(layout[0], "frames", split_axis=1, concat_axis=0, tiled=True),
            lax.all_to_all(layout[1], "frames", split_axis=1, concat_axis=0, tiled=True),
            lax.all_to_all(layout[2], "frames", split_axis=1, concat_axis=0, tiled=True),
            lax.all_to_all(layout[3], "frames", split_axis=1, concat_axis=0, tiled=True),
        )
    )
    returned = (
        lax.all_to_all(dquery, "frames", split_axis=0, concat_axis=1, tiled=True),
        lax.all_to_all(dkey, "frames", split_axis=0, concat_axis=1, tiled=True),
        lax.all_to_all(dvalue, "frames", split_axis=0, concat_axis=1, tiled=True),
    )
    grad_mixed = jnp.concatenate(
        [member.reshape(positions, inner_width) for member in returned], axis=1
    )
    gathered = (
        lax.all_gather(w_query, "frames", axis=0, tiled=True),
        lax.all_gather(w_key, "frames", axis=0, tiled=True),
        lax.all_gather(w_value, "frames", axis=0, tiled=True),
    )
    stacked = jnp.concatenate(gathered, axis=1)
    grad_normed = lax.psum_scatter(
        lax.dot_general(
            stacked, grad_mixed, (((1,), (1,)), ((), ())), preferred_element_type=jnp.float32
        ),
        "heads",
        scatter_dimension=0,
        tiled=True,
    ).T
    gain_grad = lax.psum(jnp.sum(grad_normed * values_f * inverse_rms, axis=0), "frames")
    scaled = grad_normed * gain_f
    products = lax.psum(jnp.sum(scaled * values_f, axis=1, keepdims=True), "heads")
    input_grad = (inverse_rms * scaled - values_f * inverse_rms**3 * products / D).astype(
        jnp.bfloat16
    )
    return (input_grad, gain_grad)


def solution(mesh):
    in_specs = (
        P("frames", "heads"),
        P("heads"),
        P("frames", "heads"),
        P("frames", "heads"),
        P("frames", "heads"),
        P("frames", "heads"),
    )
    out_specs = (P("frames", "heads"), P("heads"))
    return jax.shard_map(shards, mesh=mesh, in_specs=in_specs, out_specs=out_specs, check_vma=False)
```

profile of v0, /device:TPU:1, one launch (start us, length us, event | category | flops | bytes accessed | tf_op | source)
XLA Modules:
  0.0 683.0 jit_solution(18255989781953131613)
XLA Ops:
  7.2 0.7 all-gather.4.cloned.1.call-update
  7.9 0.7 all-gather.6.cloned.1.call-update
  8.7 0.7 all-gather.8.cloned.1.call-update
  9.4 1.1 copy.86
  11.0 1.4 reduce.4
  12.4 0.7 reshape.143
  13.1 18.4 %all-to-all-start.3 = ((bf16[128,2,256]{2,1,0:T(2,128)(2,1)}), bf16[128,2,256]{2,1,0:T(2,128)(2,1)S(1)}, u32[]{:S(2)}, u32[]{:S(2)}) async-start(bf16[128,2,256]{2,1,0:T(2,128)(2,1)} %reshape.143), calls=%async_computation.3 | async-start | bytes 262144 | tf_op jit(solution)/shard_map/all_to_all | solution.py:85
  31.5 1.0 copy.46
  32.6 0.7 convert_element_type.54
  33.3 9.2 %psum.21 = f32[128]{0:T(128)S(1)} all-reduce(f32[128]{0:T(128)S(1)} %fusion.18), channel_id=1, replica_groups=mesh['frames'=128,'heads'=4] {'heads'}, use_global_device_ids=true, to_apply=%region_1.0 | all-reduce | flops 128 | bytes 1024 | tf_op jit(solution)/shard_map/psum | solution.py:57
  42.6 10.3 %all_gather.18 = bf16[128,2048]{0,1:T(8,128)(2,1)S(1)} all-gather(bf16[128,512]{0,1:T(8,128)(2,1)S(1)} %fusion.20), channel_id=1, replica_groups=mesh['frames'=128,'heads'=4] {'heads'}, dimensions={1}, use_global_device_ids=true | all-gather | bytes 655360 | tf_op jit(solution)/shard_map/all_gather | solution.py:60
  52.9 47.2 %all-gather.4.cloned.1.call-done = bf16[2048,512]{1,0:T(8,128)(2,1)} async-done(((bf16[16,512]{1,0:T(8,128)(2,1)}), bf16[2048,512]{1,0:T(8,128)(2,1)}) %all-gather.4.cloned.1.call-update) | async-done | bytes 2097168 | tf_op jit(solution)/shard_map/all_gather | solution.py:97
  100.2 3.1 constant_dynamic-update-slice_fusion.2
  103.3 79.9 %all-gather.6.cloned.1.call-done = bf16[2048,512]{1,0:T(8,128)(2,1)} async-done(((bf16[16,512]{1,0:T(8,128)(2,1)}), bf16[2048,512]{1,0:T(8,128)(2,1)}) %all-gather.6.cloned.1.call-update) | async-done | bytes 2097168 | tf_op jit(solution)/shard_map/all_gather | solution.py:98
  183.1 3.2 constant_dynamic-update-slice_fusion.1
  186.3 79.8 %all-gather.8.cloned.1.call-done = bf16[2048,512]{1,0:T(8,128)(2,1)} async-done(((bf16[16,512]{1,0:T(8,128)(2,1)}), bf16[2048,512]{1,0:T(8,128)(2,1)}) %all-gather.8.cloned.1.call-update) | async-done | bytes 2097168 | tf_op jit(solution)/shard_map/all_gather | solution.py:99
  266.1 3.1 constant_dynamic-update-slice_fusion
  269.2 3.8 convolution_convert_fusion
  273.3 1.4 reduce.5
  274.7 0.7 reshape.145
  275.4 9.5 %all-to-all-start.1 = ((bf16[128,2,256]{2,1,0:T(2,128)(2,1)}), bf16[128,2,256]{2,1,0:T(2,128)(2,1)S(1)}, u32[]{:S(2)}, u32[]{:S(2)}) async-start(bf16[128,2,256]{2,1,0:T(2,128)(2,1)} %reshape.145), calls=%async_computation.1 | async-start | bytes 262144 | tf_op jit(solution)/shard_map/all_to_all | solution.py:82
  285.1 1.4 reduce.6
  286.5 0.7 reshape.147
  287.2 10.4 %all-to-all-done.1 = bf16[128,2,256]{2,1,0:T(2,128)(2,1)S(1)} async-done(((bf16[128,2,256]{2,1,0:T(2,128)(2,1)}), bf16[128,2,256]{2,1,0:T(2,128)(2,1)S(1)}, u32[]{:S(2)}, u32[]{:S(2)}) %all-to-all-start.1) | async-done | bytes 131104 | tf_op jit(solution)/shard_map/all_to_all | solution.py:82
  297.6 5.6 all-to-all-start
  303.7 1.4 reduce.8
  305.2 0.7 reshape.151
  306.1 9.9 %all-to-all-done = bf16[128,2,256]{2,1,0:T(2,128)(2,1)S(1)} async-done(((bf16[128,2,256]{2,1,0:T(2,128)(2,1)}), bf16[128,2,256]{2,1,0:T(2,128)(2,1)S(1)}, u32[]{:S(2)}, u32[]{:S(2)}) %all-to-all-start) | async-done | bytes 131104 | tf_op jit(solution)/shard_map/all_to_all | solution.py:83
  316.1 5.5 all-to-all-start.2
  322.4 0.7 reduce.7
  323.2 0.7 reshape.149
  324.0 10.4 %all-to-all-done.2 = bf16[128,2,256]{2,1,0:T(2,128)(2,1)S(1)} async-done(((bf16[128,2,256]{2,1,0:T(2,128)(2,1)}), bf16[128,2,256]{2,1,0:T(2,128)(2,1)S(1)}, u32[]{:S(2)}, u32[]{:S(2)}) %all-to-all-start.2) | async-done | bytes 131104 | tf_op jit(solution)/shard_map/all_to_all | solution.py:84
  334.4 5.6 all-to-all-start.6
  340.8 0.7 reduce.9
  341.6 0.7 reshape.153
  342.3 10.6 %all-to-all-done.6 = bf16[128,2,256]{2,1,0:T(2,128)(2,1)S(1)} async-done(((bf16[128,2,256]{2,1,0:T(2,128)(2,1)}), bf16[128,2,256]{2,1,0:T(2,128)(2,1)S(1)}, u32[]{:S(2)}, u32[]{:S(2)}) %all-to-all-start.6) | async-done | bytes 131104 | tf_op jit(solution)/shard_map/all_to_all | solution.py:91
  352.8 5.5 all-to-all-start.5
  359.4 0.7 reshape.155
  360.0 11.1 %all-to-all-done.5 = bf16[128,2,256]{2,1,0:T(2,128)(2,1)S(1)} async-done(((bf16[128,2,256]{2,1,0:T(2,128)(2,1)}), bf16[128,2,256]{2,1,0:T(2,128)(2,1)S(1)}, u32[]{:S(2)}, u32[]{:S(2)}) %all-to-all-start.5) | async-done | bytes 131104 | tf_op jit(solution)/shard_map/all_to_all | solution.py:90
  371.2 5.6 all-to-all-start.4
  377.1 12.5 %all-to-all-done.4 = bf16[128,2,256]{2,1,0:T(2,128)(2,1)S(1)} async-done(((bf16[128,2,256]{2,1,0:T(2,128)(2,1)}), bf16[128,2,256]{2,1,0:T(2,128)(2,1)S(1)}, u32[]{:S(2)}, u32[]{:S(2)}) %all-to-all-start.4) | async-done | bytes 131104 | tf_op jit(solution)/shard_map/all_to_all | solution.py:89
  389.7 5.6 fusion.12
  395.3 19.2 %reduce-scatter.2.cloned.1.call-done = f32[512,128]{1,0:T(8,128)} async-done(((f32[2048,128]{1,0:T(8,128)}), f32[512,128]{1,0:T(8,128)}) %reduce-scatter.2.cloned.1.call-update) | async-done | bytes 262160 | tf_op jit(solution)/shard_map/reduce_scatter | solution.py:102
  414.5 1.2 fusion.27
  415.7 7.1 %psum.22 = f32[128]{0:T(128)S(1)} all-reduce(f32[128]{0:T(128)S(1)} %get-tuple-element.11), channel_id=1, replica_groups=mesh['frames'=128,'heads'=4] {'heads'}, use_global_device_ids=true, to_apply=%region_6.7 | all-reduce | flops 128 | bytes 1024 | tf_op jit(solution)/shard_map/psum | solution.py:112
  422.8 1.1 fusion.24
  423.9 0.8 copy.65
  424.7 251.8 %psum.23 = f32[512]{0:T(512)} all-reduce(f32[512]{0:T(512)S(1)} %get-tuple-element.10), channel_id=1, replica_groups=mesh['frames'=128,'heads'=4] {'frames'}, use_global_device_ids=true, to_apply=%region_8.9 | all-reduce | flops 512 | bytes 4096 | tf_op jit(solution)/shard_map/psum | solution.py:110
  (39 shorter events, 5.4 us)
Async XLA Ops:
  7.2 93.0 %all-gather.4.cloned.1.call-start = ((), (), s32[]{:S(2)}) async-start(), calls=%async_computation.8 | async-start | bytes 2113536 | tf_op jit(solution)/shard_map/all_gather | solution.py:97
  7.9 175.2 %all-gather.6.cloned.1.call-start = ((), (), s32[]{:S(2)}) async-start(), calls=%async_computation.9 | async-start | bytes 2113536 | tf_op jit(solution)/shard_map/all_gather | solution.py:98
  8.6 257.5 %all-gather.8.cloned.1.call-start = ((), (), s32[]{:S(2)}) async-start(), calls=%async_computation.10 | async-start | bytes 2113536 | tf_op jit(solution)/shard_map/all_gather | solution.py:99
  13.1 262.3 %all-to-all-start.3 = ((bf16[128,2,256]{2,1,0:T(2,128)(2,1)}), bf16[128,2,256]{2,1,0:T(2,128)(2,1)S(1)}, u32[]{:S(2)}, u32[]{:S(2)}) async-start(bf16[128,2,256]{2,1,0:T(2,128)(2,1)} %reshape.143), calls=%async_computation.3 | async-start | bytes 262144 | tf_op jit(solution)/shard_map/all_to_all | solution.py:85
  275.4 22.3 %all-to-all-start.1 = ((bf16[128,2,256]{2,1,0:T(2,128)(2,1)}), bf16[128,2,256]{2,1,0:T(2,128)(2,1)S(1)}, u32[]{:S(2)}, u32[]{:S(2)}) async-start(bf16[128,2,256]{2,1,0:T(2,128)(2,1)} %reshape.145), calls=%async_computation.1 | async-start | bytes 262144 | tf_op jit(solution)/shard_map/all_to_all | solution.py:82
  297.6 18.4 %all-to-all-start = ((bf16[128,2,256]{2,1,0:T(2,128)(2,1)}), bf16[128,2,256]{2,1,0:T(2,128)(2,1)S(1)}, u32[]{:S(2)}, u32[]{:S(2)}) async-start(bf16[128,2,256]{2,1,0:T(2,128)(2,1)} %reshape.147), calls=%async_computation | async-start | bytes 262144 | tf_op jit(solution)/shard_map/all_to_all | solution.py:83
  316.1 18.4 %all-to-all-start.2 = ((bf16[128,2,256]{2,1,0:T(2,128)(2,1)}), bf16[128,2,256]{2,1,0:T(2,128)(2,1)S(1)}, u32[]{:S(2)}, u32[]{:S(2)}) async-start(bf16[128,2,256]{2,1,0:T(2,128)(2,1)} %reshape.151), calls=%async_computation.2 | async-start | bytes 262144 | tf_op jit(solution)/shard_map/all_to_all | solution.py:84
  334.4 18.4 %all-to-all-start.6 = ((bf16[128,2,256]{2,1,0:T(2,128)(2,1)}), bf16[128,2,256]{2,1,0:T(2,128)(2,1)S(1)}, u32[]{:S(2)}, u32[]{:S(2)}) async-start(bf16[128,2,256]{2,1,0:T(2,128)(2,1)} %reshape.149), calls=%async_computation.6 | async-start | bytes 262144 | tf_op jit(solution)/shard_map/all_to_all | solution.py:91
  352.8 18.4 %all-to-all-start.5 = ((bf16[128,2,256]{2,1,0:T(2,128)(2,1)}), bf16[128,2,256]{2,1,0:T(2,128)(2,1)S(1)}, u32[]{:S(2)}, u32[]{:S(2)}) async-start(bf16[128,2,256]{2,1,0:T(2,128)(2,1)} %reshape.153), calls=%async_computation.5 | async-start | bytes 262144 | tf_op jit(solution)/shard_map/all_to_all | solution.py:90
  371.2 18.4 %all-to-all-start.4 = ((bf16[128,2,256]{2,1,0:T(2,128)(2,1)}), bf16[128,2,256]{2,1,0:T(2,128)(2,1)S(1)}, u32[]{:S(2)}, u32[]{:S(2)}) async-start(bf16[128,2,256]{2,1,0:T(2,128)(2,1)} %reshape.155), calls=%async_computation.4 | async-start | bytes 262144 | tf_op jit(solution)/shard_map/all_to_all | solution.py:89
  376.7 37.7 %reduce-scatter.2.cloned.1.call-start = ((), (), s32[]{:S(2)}) async-start(), calls=%async_computation.11 | async-start | bytes 1310720 | tf_op jit(solution)/shard_map/reduce_scatter | solution.py:102
Sparse Core Ops, SparseCore 0:
  11.1 88.9 all-gather.3
  103.3 79.8 all-gather.5
  186.3 79.8 all-gather.7
  395.4 18.9 reduce-scatter.1
where the time goes:
time: 684 us; the launch traced here: 683 us
  waiting for transfers between devices  293 us (43%)
  blocking collectives  278 us (41%)
  starting transfers between devices  55.8 us (8%)
  local copies, waits for them, and re-layouts  20.1 us (3%)
  between operations  14.1 us (2%)
  other arithmetic  11 us (2%)
  matrix products  10.6 us (2%)
    psum x1, blocking collectives, shards(): lax.psum(jnp.sum(grad_normed * values_f * inverse_rms, axis=0), 'frames')  252 us
    all_gather x1, waiting for transfers between devices, shards(): lax.all_gather(w_key, 'frames', axis=0, tiled=True)  79.9 us
    all_gather x1, waiting for transfers between devices, shards(): lax.all_gather(w_value, 'frames', axis=0, tiled=True)  79.8 us
    all_gather x1, waiting for transfers between devices, shards(): lax.all_gather(w_query, 'frames', axis=0, tiled=True)  47.2 us
    reduce_scatter x1, waiting for transfers between devices, shards(): lax.psum_scatter(lax.dot_general(stacked, grad_mixed, (((1,), (1,)), ((),...  19.2 us
    all_to_all x1, starting transfers between devices, shards(): lax.all_to_all(layout[3], 'frames', split_axis=1, concat_axis=0, tiled=True)  18.4 us
    unnamed x25, local copies, waits for them, and re-layouts  14.5 us
  transfers between devices with their start and end apart: 11, of which 10 were waited for; matrix products, arithmetic and copies ran while one was open for 5% of the time, Pallas kernels for 0%

commit v1 on v0

v1 whole, which is shorter than its diff:
```python
import functools

import jax
import jax.numpy as jnp
from jax import lax
from jax.experimental import pallas as pl
from jax.experimental.pallas import tpu as pltpu
from jax.sharding import PartitionSpec as P

EPS = 1e-05
HDIM = 128
F32 = jnp.float32
BF16 = jnp.bfloat16
NT = (((1,), (1,)), ((), ()))
TN = (((0,), (0,)), ((), ()))


def dot(a, b, dims=(((1,), (0,)), ((), ()))):
    return lax.dot_general(a, b, dims, preferred_element_type=F32)


def kernel(
    nz, ny, nx,
    a_ref, gain_ref, wq_ref, wk_ref, wv_ref, og_ref,
    out_ref, gg_ref,
    w0, w1, stage, za, zg, sa, sg, xf, nrm, ogf, gmix,
    gains, gsum, gpart, gx, gy, gz, gsend, ig, part, xsend, xrecv, ysend, yrecv, zsend, zrecv,
    w_s, w_r, p1_s, p1_r, p2_s, p2_r, az_s, az_r, ay_s, ay_r, ax_s, ax_r, ac_s, ac_r,
    oc_s, oc_r, gn_s, gn_r, pr_s, pr_r, xs_s, xs_r, gp_s, gp_r, gx_s, gx_r, gy_s, gy_r, gz_s, gz_r,
    oy_s, oy_r, oz_s, oz_r,
):
    frame = lax.axis_index("frames")
    x = lax.axis_index("heads")
    c = lax.rem(frame, 2)
    y = lax.rem(lax.div(frame, 2), ny)
    z = lax.div(frame, 2 * ny)
    chip = z * ny + y
    width = a_ref.shape[1]
    model = width * nx
    tokens = 2 * nz * ny
    zrows = 2 * ny
    yrows = 2 * nz
    wrows = wq_ref.shape[0]
    crows = 2 * wrows
    ws = (w0, w1)

    def dev(z_, y_, c_, x_):
        return ((z_ * ny + y_) * 2 + c_, x_)

    def rcopy(src, dst, ssem, rsem, to):
        return pltpu.make_async_remote_copy(
            src_ref=src, dst_ref=dst, send_sem=ssem, recv_sem=rsem,
            device_id=to, device_id_type=pl.DeviceIdType.MESH,
        )

    def wrap(v, n):
        return lax.rem(v + 2 * n, n)

    def mult(v, m):
        return pl.multiple_of(v * m, m)

    mate = dev(z, y, 1 - c, x)
    own_rows = pl.ds(mult(c, tokens), tokens)
    mate_rows = pl.ds(mult(1 - c, tokens), tokens)

    def yp(o):
        return wrap(y + o, ny)

    def zp(o):
        return wrap(z + o, nz)

    def xp(o):
        return wrap(x + o, nx)

    bar = pltpu.get_barrier_semaphore()

    def hello(to):
        pl.semaphore_signal(bar, inc=1, device_id=to, device_id_type=pl.DeviceIdType.MESH)

    hello(mate)
    for o in range(1, ny):
        hello(dev(z, yp(o), c, x))
    for o in range(1, nz):
        hello(dev(zp(o), y, c, x))
    for o in range(1, nx):
        hello(dev(z, y, c, xp(o)))
    pl.semaphore_wait(bar, 1 + (ny - 1) + (nz - 1) + (nx - 1))

    def z_send(src, dst, s, r):
        def copy(o):
            to = zp(o)
            return rcopy(
                src.at[pl.ds(mult(to, zrows), zrows)], dst.at[pl.ds(mult(z, zrows), zrows)],
                s.at[to], r.at[z], dev(to, y, c, x),
            )
        return copy

    def z_wait(dst, s, r, o):
        at = zp(o)
        ref = dst.at[pl.ds(mult(at, zrows), zrows)]
        rcopy(ref, ref, s.at[at], r.at[at], dev(at, y, c, x)).wait_recv()

    def y_send(src, dst, dst_base, dst_cols, s, r):
        def copy(o):
            to = yp(o)
            return rcopy(
                src.at[pl.ds(mult(to, yrows), yrows)],
                dst.at[pl.ds(pl.multiple_of(dst_base + y * yrows, yrows), yrows), dst_cols],
                s.at[to], r.at[y], dev(z, to, c, x),
            )
        return copy

    def y_wait(dst, dst_base, dst_cols, s, r, o):
        at = yp(o)
        ref = dst.at[pl.ds(pl.multiple_of(dst_base + at * yrows, yrows), yrows), dst_cols]
        rcopy(ref, ref, s.at[at], r.at[at], dev(z, at, c, x)).wait_recv()

    def swapped(value, na, nb):
        i = lax.broadcasted_iota(jnp.int32, (tokens, tokens), 0)
        j = lax.broadcasted_iota(jnp.int32, (tokens, tokens), 1)
        b = lax.div(i, 2 * na)
        a = lax.rem(lax.div(i, 2), na)
        pair = lax.rem(i, 2)
        hot = jnp.where(j == (a * nb + b) * 2 + pair, 1.0, 0.0).astype(BF16)
        return dot(hot, value).astype(BF16)

    own_cols = pl.ds(mult(x, width), width)
    all_cols = pl.ds(0, width)

    az = z_send(a_ref, za, az_s, az_r)
    for o in range(1, nz):
        az(o).start()

    for j in range(2):
        for i, w_ref in enumerate((wq_ref, wk_ref, wv_ref)):
            mine = pl.ds(mult(2 * c + j, HDIM), HDIM)
            theirs = pl.ds(mult(2 * (1 - c) + j, HDIM), HDIM)
            ws[j][pl.ds(pl.multiple_of(chip * crows + c * wrows, wrows), wrows), i * HDIM:(i + 1) * HDIM] = w_ref[:, mine]
            stage[j, :, i * HDIM:(i + 1) * HDIM] = w_ref[:, theirs]

    def w_mate(j, core):
        return rcopy(
            stage.at[j], ws[j].at[pl.ds(pl.multiple_of(chip * crows + core * wrows, wrows), wrows)],
            w_s.at[j], w_r.at[j], mate,
        )

    for j in range(2):
        w_mate(j, c).start()

    gains[x] = gain_ref[...].astype(F32)

    def gain_copy(o):
        return rcopy(gains.at[x], gains.at[x], gn_s.at[xp(o)], gn_r.at[x], dev(z, y, c, xp(o)))

    for o in range(1, nx):
        gain_copy(o).start()

    def block(zb, yb):
        return pl.ds(mult(zb * ny + yb, crows), crows)

    def p1(j, o):
        ref = ws[j].at[block(z, y)]
        to = dev(z, yp(o), c, x) if j == 0 else dev(zp(o), y, c, x)
        return rcopy(ref, ref, p1_s.at[j, o], p1_r.at[j, o], to)

    def p1_wait(j, o):
        ref = ws[j].at[block(z, yp(-o)) if j == 0 else block(zp(-o), y)]
        rcopy(ref, ref, p1_s.at[j, o], p1_r.at[j, o], mate).wait_recv()

    def place(j, d, age, k):
        sign = 1 if d == 0 else -1
        if j == 0:
            return ws[0].at[block(zp(-sign * age), wrap(y - k, ny))]
        return ws[1].at[block(wrap(z - k, nz), yp(-sign * age))]

    def p2(j, d, age, k):
        sign = 1 if d == 0 else -1
        to = dev(zp(sign), y, c, x) if j == 0 else dev(z, yp(sign), c, x)
        ref = place(j, d, age, k)
        return rcopy(ref, ref, p2_s.at[j, d, age, k], p2_r.at[j, d, age, k], to)

    def p2_wait(j, d, age, k):
        ref = place(j, d, age + 1, k)
        rcopy(ref, ref, p2_s.at[j, d, age, k], p2_r.at[j, d, age, k], mate).wait_recv()

    ring = nz
    subs = ny
    last = ring // 2 - 1

    def goes(d, age, k):
        if age < last:
            return True
        if age > last:
            return False
        return (k < subs // 2) if d == 0 else (k >= subs // 2)

    for j in range(2):
        w_mate(j, 1 - c).wait_recv()
    for d in range(2):
        if goes(d, 0, 0):
            for j in range(2):
                p2(j, d, 0, 0).start()
    order = sorted(range(1, ny), key=lambda o: min(o, ny - o))
    for o in order:
        for j in range(2):
            p1(j, o).start()

    za[pl.ds(mult(z, zrows), zrows), :] = a_ref[pl.ds(mult(z, zrows), zrows), :]
    for o in range(1, nz):
        z_wait(za, az_s, az_r, o)
    sa[...] = swapped(za[...], nz, ny)
    ay = y_send(sa, xf, c * tokens, own_cols, ay_s, ay_r)
    for o in range(1, ny):
        ay(o).start()
    xf[pl.ds(pl.multiple_of(c * tokens + y * yrows, yrows), yrows), own_cols] = sa[pl.ds(mult(y, yrows), yrows), :]

    for k in order:
        for j in range(2):
            p1_wait(j, k)
            for d in range(2):
                if goes(d, 0, k):
                    p2(j, d, 0, k).start()

    for o in range(1, ny):
        y_wait(xf, c * tokens, own_cols, ay_s, ay_r, o)

    def xcols(at):
        return pl.ds(mult(at, width), width)

    def ax(o):
        ref = xf.at[own_rows, own_cols]
        return rcopy(ref, ref, ax_s.at[xp(o)], ax_r.at[x], dev(z, y, c, xp(o)))

    def ac(at):
        ref = xf.at[own_rows, xcols(at)]
        return rcopy(ref, ref, ac_s.at[at], ac_r.at[at], mate)

    for o in (2, 1, 3)[-(nx - 1):] if nx == 4 else range(1, nx):
        ax(o).start()
    ac(x).start()

    oz = z_send(og_ref, zg, oz_s.at[0], oz_r.at[0])
    for o in range(1, nz):
        oz(o).start()

    def hop(age):
        @pl.loop(0, subs // 2)
        def _(k):
            for j in range(2):
                for d in range(2):
                    p2_wait(j, d, age - 1, k)
                    if goes(d, age, 0):
                        p2(j, d, age, k).start()

        @pl.loop(subs // 2, subs)
        def _(k):
            for j in range(2):
                for d in range(2):
                    p2_wait(j, d, age - 1, k)
                    if goes(d, age, subs - 1):
                        p2(j, d, age, k).start()

    if last >= 1:
        hop(1)

    zg[pl.ds(mult(z, zrows), zrows), :] = og_ref[pl.ds(mult(z, zrows), zrows), :]
    for o in range(1, nz):
        z_wait(zg, oz_s.at[0], oz_r.at[0], o)
    sg[0] = swapped(zg[...], nz, ny)
    oy = y_send(sg.at[0], sg.at[1], 0, all_cols, oy_s.at[0], oy_r.at[0])
    for o in range(1, ny):
        oy(o).start()
    sg[1, pl.ds(mult(y, yrows), yrows), :] = sg[0, pl.ds(mult(y, yrows), yrows), :]

    for o in range(1, nx):
        at = xp(o)
        ref = xf.at[own_rows, xcols(at)]
        rcopy(ref, ref, ax_s.at[at], ax_r.at[at], mate).wait_recv()
        ac(at).start()

    if last >= 2:
        hop(2)

    for o in range(1, ny):
        y_wait(sg.at[1], 0, all_cols, oy_s.at[0], oy_r.at[0], o)

    def oc(core):
        cols = pl.ds(mult(1 - core, 2 * HDIM), 2 * HDIM)
        return rcopy(
            sg.at[1, :, cols], ogf.at[pl.ds(mult(core, tokens), tokens)], oc_s, oc_r, mate,
        )

    oc(c).start()
    ogf[own_rows, :] = sg[1, :, pl.ds(mult(c, 2 * HDIM), 2 * HDIM)]

    for at in range(nx):
        ref = xf.at[mate_rows, at * width:(at + 1) * width]
        rcopy(ref, ref, ac_s.at[at], ac_r.at[at], mate).wait_recv()
    for o in range(1, nx):
        at = xp(o)
        rcopy(gains.at[at], gains.at[at], gn_s.at[at], gn_r.at[at], mate).wait_recv()
    square_sum = jnp.zeros((2 * tokens, 1), F32)
    for at in range(nx):
        act = xf[:, at * width:(at + 1) * width].astype(F32)
        square_sum += jnp.sum(act * act, axis=1, keepdims=True)
    inverse_rms = lax.rsqrt(square_sum / model + EPS)
    for at in range(nx):
        act = xf[:, at * width:(at + 1) * width].astype(F32)
        nrm[:, at * width:(at + 1) * width] = (act * inverse_rms * gains[at]).astype(BF16)

    if last >= 3:
        hop(3)

    rcopy(sg.at[1, :, 0:2 * HDIM], ogf.at[mate_rows], oc_s, oc_r, mate).wait_recv()

    @pl.loop(0, subs // 2)
    def _(k):
        for j in range(2):
            p2_wait(j, 0, last, k)

    @pl.loop(subs // 2, subs)
    def _(k):
        for j in range(2):
            p2_wait(j, 1, last, k)

    i = lax.broadcasted_iota(jnp.int32, (2 * tokens, 1), 0)
    j = lax.broadcasted_iota(jnp.int32, (1, 2 * tokens), 1)

    def frame_of(r):
        core = lax.div(r, tokens)
        yy = lax.rem(lax.div(r, yrows), ny)
        zz = lax.rem(lax.div(r, 2), nz)
        return (zz * ny + yy) * 2 + core

    causal = (frame_of(i) >= frame_of(j)) & (lax.rem(i, 2) == lax.rem(j, 2))
    scale = HDIM ** (-0.5)
    inner = jnp.zeros((2 * tokens, 1), F32)
    for h in range(2):
        proj = dot(nrm[...], ws[h][...])
        low = proj.astype(BF16)
        q, k, v = low[:, :HDIM], low[:, HDIM:2 * HDIM], low[:, 2 * HDIM:]
        g = ogf[:, h * HDIM:(h + 1) * HDIM]
        scores = dot(q, k, NT) * scale
        exps = jnp.where(causal, jnp.exp(jnp.where(causal, scores, 0.0)), 0.0)
        probs = exps / jnp.sum(exps, axis=1, keepdims=True)
        dprobs = dot(g, v, NT)
        delta = jnp.sum(probs * dprobs, axis=1, keepdims=True)
        dscores = (probs * (dprobs - delta) * scale).astype(BF16)
        gq = dot(dscores, k).astype(BF16)
        gk = dot(dscores, q, TN).astype(BF16)
        gv = dot(probs.astype(BF16), g, TN).astype(BF16)
        for n, part_of in enumerate((gq, gk, gv)):
            gmix[h, :, n * HDIM:(n + 1) * HDIM] = part_of
            inner += jnp.sum(part_of.astype(F32) * proj[:, n * HDIM:(n + 1) * HDIM], axis=1, keepdims=True)
    inner = inner / model

    xorder = (2, 1, 3, 0) if nx == 4 else tuple(range(1, nx)) + (0,)

    def pr(b, core):
        return rcopy(
            ig.at[b, pl.ds(mult(1 - core, tokens), tokens)], part.at[b], pr_s.at[b], pr_r.at[b], mate,
        )

    def xs(b, o):
        return rcopy(xsend.at[b], xrecv.at[b], xs_s.at[b], xs_r.at[b], dev(z, y, c, xp(o)))

    def forward(b):
        pr(b, 1 - c).wait_recv()
        total = ig[b, own_rows, :] + part[b]
        if b < nx - 1:
            xsend[b] = total.astype(BF16)
            xs(b, xorder[b]).start()
        else:
            ig[b, own_rows, :] = total

    for b, o in enumerate(xorder):
        at = xp(o)
        feats = pl.ds(mult(at, width), width)
        gn = dot(gmix[0], w0[feats, :], NT) + dot(gmix[1], w1[feats, :], NT)
        act = xf[:, feats].astype(F32) * inverse_rms
        gsum[at] = jnp.sum(gn * act, axis=0, keepdims=True)
        ig[b] = inverse_rms * (gn * gains[at] - act * inner)
        pr(b, c).start()
        if b > 0:
            forward(b - 1)
    gp = rcopy(gsum, gpart, gp_s, gp_r, mate)
    gp.start()
    forward(nx - 1)
    gp.wait_recv()
    gp.wait_send()
    gsum[...] += gpart[...]

    def gxc(o):
        return rcopy(gsum.at[xp(o)], gx.at[x], gx_s.at[xp(o)], gx_r.at[x], dev(z, y, c, xp(o)))

    for o in range(1, nx):
        gxc(o).start()
    gx[x] = gsum[x]

    total = ig[nx - 1, own_rows, :]
    for b in range(nx - 1):
        xs(b, xorder[b]).wait_recv()
        total += xrecv[b].astype(F32)
    ysend[...] = total.astype(BF16)
    by = y_send(ysend, yrecv, 0, all_cols, oy_s.at[1], oy_r.at[1])
    for o in range(1, ny):
        by(o).start()
    for o in range(1, nx):
        at = xp(o)
        rcopy(gx.at[at], gx.at[at], gx_s.at[at], gx_r.at[at], mate).wait_recv()
    gsend[0] = jnp.sum(gx[...], axis=0)
    gy[y] = gsend[0]

    def gyc(o):
        return rcopy(gsend.at[0], gy.at[y], gy_s.at[yp(o)], gy_r.at[y], dev(z, yp(o), c, x))

    def gzc(o):
        return rcopy(gsend.at[1], gz.at[z], gz_s.at[zp(o)], gz_r.at[z], dev(zp(o), y, c, x))

    for o in range(1, ny):
        gyc(o).start()
    yrecv[pl.ds(mult(y, yrows), yrows), :] = ysend[pl.ds(mult(y, yrows), yrows), :]
    for o in range(1, ny):
        y_wait(yrecv, 0, all_cols, oy_s.at[1], oy_r.at[1], o)
    zsend[...] = swapped(yrecv[...], ny, nz)
    bz = z_send(zsend, zrecv, oz_s.at[1], oz_r.at[1])
    for o in range(1, nz):
        bz(o).start()
    for o in range(1, ny):
        at = yp(o)
        rcopy(gy.at[at], gy.at[at], gy_s.at[at], gy_r.at[at], mate).wait_recv()
    gsend[1] = jnp.sum(gy[...], axis=0)
    gz[z] = gsend[1]
    for o in range(1, nz):
        gzc(o).start()
    zrecv[pl.ds(mult(z, zrows), zrows), :] = zsend[pl.ds(mult(z, zrows), zrows), :]

    for j in range(2):
        w_mate(j, c).wait_send()
        for o in range(1, ny):
            p1(j, o).wait_send()
    for age in range(last + 1):
        for half in range(2):
            @pl.loop(half * (subs // 2), (half + 1) * (subs // 2))
            def _(k):
                for j in range(2):
                    for d in range(2):
                        if goes(d, age, half * (subs - 1)):
                            p2(j, d, age, k).wait_send()
    for o in range(1, nz):
        az(o).wait_send()
        oz(o).wait_send()
    for o in range(1, ny):
        ay(o).wait_send()
        oy(o).wait_send()
        by(o).wait_send()
        gyc(o).wait_send()
    for o in range(1, nx):
        gain_copy(o).wait_send()
        ax(o).wait_send()
        gxc(o).wait_send()
    for at in range(nx):
        ac(at).wait_send()
    oc(c).wait_send()
    for b, o in enumerate(xorder):
        pr(b, c).wait_send()
        if b < nx - 1:
            xs(b, o).wait_send()

    for o in range(1, nz):
        z_wait(zrecv, oz_s.at[1], oz_r.at[1], o)
    out_ref[...] = zrecv[...]
    for o in range(1, nz):
        at = zp(o)
        rcopy(gz.at[at], gz.at[at], gz_s.at[at], gz_r.at[at], mate).wait_recv()
    gg_ref[...] = jnp.sum(gz[...], axis=0)
    for o in range(1, nz):
        bz(o).wait_send()
        gzc(o).wait_send()


def shards(nz, ny, nx, activations, norm_gain, w_query, w_key, w_value, out_grad):
    tokens, width = activations.shape
    model = width * nx
    wcols = 3 * HDIM
    wrows = w_query.shape[0]
    vmem = pl.BlockSpec(memory_space=pltpu.VMEM)
    dma = pltpu.SemaphoreType.DMA
    ring = nz // 2
    scratch = [
        pltpu.VMEM((model, wcols), BF16),
        pltpu.VMEM((model, wcols), BF16),
        pltpu.VMEM((2, wrows, wcols), BF16),
        pltpu.VMEM((tokens, width), BF16),
        pltpu.VMEM((tokens, width), BF16),
        pltpu.VMEM((tokens, width), BF16),
        pltpu.VMEM((2, tokens, width), BF16),
        pltpu.VMEM((2 * tokens, model), BF16),
        pltpu.VMEM((2 * tokens, model), BF16),
        pltpu.VMEM((2 * tokens, 2 * HDIM), BF16),
        pltpu.VMEM((2, 2 * tokens, wcols), BF16),
        pltpu.VMEM((nx, 1, width), F32),
        pltpu.VMEM((nx, 1, width), F32),
        pltpu.VMEM((nx, 1, width), F32),
        pltpu.VMEM((nx, 1, width), F32),
        pltpu.VMEM((ny, 1, width), F32),
        pltpu.VMEM((nz, 1, width), F32),
        pltpu.VMEM((2, 1, width), F32),
        pltpu.VMEM((nx, 2 * tokens, width), F32),
        pltpu.VMEM((nx, tokens, width), F32),
        pltpu.VMEM((nx, tokens, width), BF16),
        pltpu.VMEM((nx, tokens, width), BF16),
        pltpu.VMEM((tokens, width), BF16),
        pltpu.VMEM((tokens, width), BF16),
        pltpu.VMEM((tokens, width), BF16),
        pltpu.VMEM((tokens, width), BF16),
    ]
    for shape in (
        (2,), (2, ny), (2, 2, ring, ny), (nz,), (ny,), (nx,), (nx,),
        (), (nx,), (nx,), (nx,), (), (nx,), (ny,), (nz,),
        (2, ny), (2, nz),
    ):
        scratch += [dma(shape), dma(shape)] if shape else [dma, dma]
    out, gain = pl.pallas_call(
        functools.partial(kernel, nz, ny, nx),
        out_shape=(
            jax.ShapeDtypeStruct((tokens, width), BF16),
            jax.ShapeDtypeStruct((1, width), F32),
        ),
        in_specs=[vmem] * 6,
        out_specs=(vmem, vmem),
        scratch_shapes=scratch,
        compiler_params=pltpu.CompilerParams(
            collective_id=0, has_side_effects=True, vmem_limit_bytes=48 * 1024 * 1024
        ),
    )(activations, norm_gain.reshape(1, width), w_query, w_key, w_value, out_grad)
    return out, gain.reshape(width)


def solution(mesh, nz=8, ny=8):
    nx = mesh.shape["heads"]
    in_specs = (
        P("frames", "heads"),
        P("heads"),
        P("frames", "heads"),
        P("frames", "heads"),
        P("frames", "heads"),
        P("frames", "heads"),
    )
    out_specs = (P("frames", "heads"), P("heads"))
    return jax.shard_map(
        functools.partial(shards, nz, ny, nx),
        mesh=mesh, in_specs=in_specs, out_specs=out_specs, check_vma=False,
    )
```

time: 684 us -> 80.3 us (0.12)
  waiting for transfers between devices: 293 us -> 0 us
  blocking collectives: 278 us -> 0 us
  Pallas kernels: 0 us -> 72.9 us
  starting transfers between devices: 55.8 us -> 0 us
  local copies, waits for them, and re-layouts: 20.1 us -> 5.88 us
  between operations: 14.1 us -> 0.64 us
  other arithmetic: 11 us -> 0 us
  matrix products: 10.6 us -> 0 us
    psum x3 -> x0, blocking collectives: 268 us -> none  [the longest x1 252 us: shards(): lax.psum(jnp.sum(grad_normed * values_f * inverse_rms, axis=0), 'frames')]
    all_gather x3 -> x0, waiting for transfers between devices: 207 us -> none  [the longest x1 79.9 us: shards(): lax.all_gather(w_key, 'frames', axis=0, tiled=True)]
    pallas_call x0 -> x1, Pallas kernels: none -> 72.9 us  [shards(): pl.pallas_call(functools.partial(kernel, nz, ny, nx), out_shape=(jax.Shap...]
    all_to_all x7 -> x0, waiting for transfers between devices: 65 us -> none  [the longest x1 12.5 us: shards(): lax.all_to_all(dquery, 'frames', split_axis=0, concat_axis=1, tiled=True)]
    all_to_all x7 -> x0, starting transfers between devices: 55.6 us -> none  [the longest x1 18.4 us: shards(): lax.all_to_all(layout[3], 'frames', split_axis=1, concat_axis=0, tiled=True)]
    reduce_scatter x1 -> x0, waiting for transfers between devices: 19.2 us -> none  [shards(): lax.psum_scatter(lax.dot_general(stacked, grad_mixed, (((1,), (1,)), ((),...]
    dot_general x7 -> x0, matrix products: 10.6 us -> none  [the longest x1 5.58 us: shards(): lax.dot_general(stacked, grad_mixed, (((1,), (1,)), ((), ())), preferred_...]
    all_gather x1 -> x0, blocking collectives: 10.3 us -> none  [shards(): normed = lax.all_gather(normed_own, 'heads', axis=1, tiled=True)]
  transfers between devices with their start and end apart: 11 -> 0, of which waited for: 10 -> 0; matrix products, arithmetic and copies ran while one was open for 5% -> 0% of each run, Pallas kernels for 0% -> 0%
where the time goes in v1:
time: 80.3 us; the launch traced here: 79.4 us
  Pallas kernels  72.9 us (91%)
  local copies, waits for them, and re-layouts  5.88 us (7%)
    pallas_call x1, Pallas kernels, shards(): pl.pallas_call(functools.partial(kernel, nz, ny, nx), out_shape=(jax.Shap...  72.9 us
    unnamed x12, local copies, waits for them, and re-layouts  5.19 us

profile of v1, /device:TPU:1, one launch (start us, length us, event | category | flops | bytes accessed | tf_op | source)
XLA Modules:
  0.0 79.4 jit_solution(10510812687966395073)
XLA Ops:
  0.6 0.7 reshape.10.gain_ref
  1.3 0.0 copy-start
  1.3 0.9 %copy-done = bf16[128,512]{1,0:T(8,128)(2,1)S(1)} copy-done((bf16[128,512]{1,0:T(8,128)(2,1)S(1)}, bf16[128,512]{1,0:T(8,128)(2,1)}, u32[]{:S(2)}) %copy-start) | copy-done | bytes 131096
  2.2 0.0 copy-start.1
  2.2 0.9 %copy-done.1 = bf16[128,512]{1,0:T(8,128)(2,1)S(1)} copy-done((bf16[128,512]{1,0:T(8,128)(2,1)S(1)}, bf16[128,512]{1,0:T(8,128)(2,1)}, u32[]{:S(2)}) %copy-start.1) | copy-done | bytes 131096
  3.1 0.0 copy-start.2
  3.1 0.7 copy-done.2
  3.8 0.0 copy-start.3
  3.8 0.7 copy-done.3
  4.6 0.0 copy-start.4
  4.6 0.7 copy-done.4
  5.3 72.9 %shard_map.77 = (bf16[128,512]{1,0:T(8,128)(2,1)S(1)}, f32[1,512]{1,0:T(1,128)S(1)}) custom-call(bf16[128,512]{1,0:T(8,128)(2,1)S(1)} %copy-done, bf16[1,512]{1,0:T(2,128)(2,1)S(1)} %reshape.10.gain_ref, bf16[16,512]{1,0:T(8,128)(2,1)S(1)} %copy-done.2, bf16[16,512]{1,0:T(8,128)(2,1)S(1)} %copy-done.3, bf16[16,512]{1,0:T(8,128)(2,1)S(1)} %copy-done.4, ...), custom_call_target="tpu_custom_call" | custom-call | tf_op jit(solution)/shard_map/pallas_call | solution.py:524
  78.2 0.7 copy.10
  78.8 0.6 copy.11
Async XLA Ops:
  1.3 0.9 %copy-start = (bf16[128,512]{1,0:T(8,128)(2,1)S(1)}, bf16[128,512]{1,0:T(8,128)(2,1)}, u32[]{:S(2)}) copy-start(bf16[128,512]{1,0:T(8,128)(2,1)} %a_ref.1) | copy-start | bytes 393220
  2.2 0.9 %copy-start.1 = (bf16[128,512]{1,0:T(8,128)(2,1)S(1)}, bf16[128,512]{1,0:T(8,128)(2,1)}, u32[]{:S(2)}) copy-start(bf16[128,512]{1,0:T(8,128)(2,1)} %og_ref.1) | copy-start | bytes 393220
  3.1 0.7 copy-start.2
  3.8 0.7 copy-start.3
  4.6 0.7 copy-start.4

commit v2 on v0

v2 whole, which is shorter than its diff:
```python
import functools

import jax
import jax.numpy as jnp
from jax import lax
from jax.experimental import pallas as pl
from jax.experimental.pallas import tpu as pltpu
from jax.sharding import PartitionSpec as P

EPS = 1e-05
HDIM = 128
F32 = jnp.float32
BF16 = jnp.bfloat16
NT = (((1,), (1,)), ((), ()))
TN = (((0,), (0,)), ((), ()))


def dot(a, b, dims=(((1,), (0,)), ((), ()))):
    return lax.dot_general(a, b, dims, preferred_element_type=F32)


def kernel(
    nz, ny, nx,
    a_ref, gain_ref, wq_ref, wk_ref, wv_ref, og_ref,
    out_ref, gg_ref,
    w0, w1, za, zg, sa, sg, xf, nrm, ogf, gmix,
    gains, gsum, gpart, gx, gy, gz, gsend, ig, part, xsend, xrecv, ysend, yrecv, zsend, zrecv,
    gain_low, l_s, w_s, w_r, p1_s, p1_r, p2_s, p2_r, az_s, az_r, ay_s, ay_r, ax_s, ax_r, ac_s, ac_r,
    oc_s, oc_r, gn_s, gn_r, pr_s, pr_r, xs_s, xs_r, gp_s, gp_r, gx_s, gx_r, gy_s, gy_r, gz_s, gz_r,
    oy_s, oy_r, oz_s, oz_r,
):
    frame = lax.axis_index("frames")
    x = lax.axis_index("heads")
    c = frame & 1
    y = (frame >> 1) & (ny - 1)
    z = frame >> (ny.bit_length())
    chip = z * ny + y
    width = a_ref.shape[1]
    model = width * nx
    tokens = 2 * nz * ny
    zrows = 2 * ny
    yrows = 2 * nz
    wrows = wq_ref.shape[0]
    crows = 2 * wrows
    ws = (w0, w1)

    def dev(z_, y_, c_, x_):
        return ((z_ * ny + y_) * 2 + c_, x_)

    def rcopy(src, dst, ssem, rsem, to):
        return pltpu.make_async_remote_copy(
            src_ref=src, dst_ref=dst, send_sem=ssem, recv_sem=rsem,
            device_id=to, device_id_type=pl.DeviceIdType.MESH,
        )

    def wrap(v, n):
        return v & (n - 1)

    def rows(v, m):
        return pl.ds(pl.multiple_of(v * m, m), m)

    def block(zb, yb):
        return rows(zb * ny + yb, crows)

    mate = dev(z, y, 1 - c, x)
    own_rows, mate_rows = rows(c, tokens), rows(1 - c, tokens)
    own_cols, all_cols = rows(x, width), pl.ds(0, width)

    def yp(o):
        return wrap(y + o, ny)

    def zp(o):
        return wrap(z + o, nz)

    def xp(o):
        return wrap(x + o, nx)

    def far(n):
        return sorted(range(1, n), key=lambda o: -min(o, n - o))

    arriving, leaving, local = {}, [], []

    def sent(copies):
        for copy in copies:
            copy.start()

    def expect(name, *waits):
        arriving[name] = waits

    def arrived(name):
        for wait in arriving.pop(name):
            wait()

    def landing(ref, rsem):
        return lambda: rcopy(ref, ref, rsem, rsem, mate).wait_recv()

    def left(ref, ssem):
        leaving.append(lambda: rcopy(ref, ref, ssem, ssem, mate).wait_send())

    def z_step(name, src, dst, s, r):
        sent(
            rcopy(src.at[rows(zp(o), zrows)], dst.at[rows(z, zrows)], s, r, dev(zp(o), y, c, x))
            for o in far(nz)
        )
        bulk = dst.at[pl.ds(0, (nz - 1) * zrows)]
        left(bulk, s)
        expect(name, landing(bulk, r))

    def y_step(name, src, dst, base, cols, s, r, by_piece=False):
        def place(at):
            return dst.at[pl.ds(pl.multiple_of(base + at * yrows, yrows), yrows), cols]

        sent(
            rcopy(
                src.at[rows(yp(o), yrows)], place(y), s, r.at[y] if by_piece else r, dev(z, yp(o), c, x)
            )
            for o in far(ny)
        )
        bulk = src.at[pl.ds(0, (ny - 1) * yrows)]
        left(bulk, s)
        if not by_piece:
            expect(name, landing(bulk, r))

    def swapped(value, na, nb):
        i = lax.broadcasted_iota(jnp.int32, (tokens, tokens), 0)
        j = lax.broadcasted_iota(jnp.int32, (tokens, tokens), 1)
        b = lax.div(i, 2 * na)
        a = lax.rem(lax.div(i, 2), na)
        hot = jnp.where(j == (a * nb + b) * 2 + lax.rem(i, 2), 1.0, 0.0).astype(BF16)
        return dot(hot, value).astype(BF16)

    def p1(j, o):
        ref = ws[j].at[block(z, y)]
        to = dev(z, yp(o), c, x) if j == 0 else dev(zp(o), y, c, x)
        return rcopy(ref, ref, p1_s.at[j, 0], p1_r.at[j, o], to)

    def p1_wait(j, o):
        landing(ws[j].at[block(z, yp(-o)) if j == 0 else block(zp(-o), y)], p1_r.at[j, o])()

    def place(j, d, age, k):
        sign = 1 if d == 0 else -1
        if j == 0:
            return ws[0].at[block(zp(-sign * age), wrap(y - k, ny))]
        return ws[1].at[block(wrap(z - k, nz), yp(-sign * age))]

    def p2(j, d, age, k):
        sign = 1 if d == 0 else -1
        to = dev(zp(sign), y, c, x) if j == 0 else dev(z, yp(sign), c, x)
        ref = place(j, d, age, k)
        return rcopy(ref, ref, p2_s.at[j, 0, 0, 0], p2_r.at[j, d, age, k], to)

    subs = ny
    last = nz // 2 - 1

    def goes(d, age, k):
        if age != last:
            return age < last
        return (k < subs // 2) if d == 0 else (k >= subs // 2)

    def each(act, halves=(0, 1)):
        for half in halves:
            @pl.loop(half * (subs // 2), (half + 1) * (subs // 2))
            def _(k):
                for j in range(2):
                    for d in range(2):
                        act(j, d, k, half * (subs - 1))

    def hop(age, halves=(0, 1)):
        def act(j, d, k, kind):
            if goes(d, age - 1, kind):
                landing(place(j, d, age, k), p2_r.at[j, d, age - 1, k])()
            if goes(d, age, kind):
                p2(j, d, age, k).start()

        each(act, halves)

    order = sorted(range(1, ny), key=lambda o: min(o, ny - o))

    def to_here(src, dst, n):
        copy = pltpu.make_async_copy(src, dst, l_s.at[n])
        copy.start()
        local.append(copy.wait)

    state = {}

    def drain():
        while leaving:
            leaving.pop(0)()

    def begin():
        for j in range(2):
            for i, w_ref in enumerate((wq_ref, wk_ref, wv_ref)):
                to_here(
                    w_ref.at[:, rows(2 * c + j, HDIM)],
                    ws[j].at[rows(2 * chip + c, wrows), i * HDIM:(i + 1) * HDIM],
                    3 * j + i,
                )
        to_here(a_ref.at[rows(z, zrows)], za.at[rows(z, zrows)], 6)
        to_here(og_ref.at[rows(z, zrows)], zg.at[rows(z, zrows)], 7)
        to_here(gain_ref, gain_low, 8)

        peers = [mate]
        peers += [dev(z, yp(o), c, x) for o in range(1, ny)]
        peers += [dev(zp(o), y, c, x) for o in range(1, nz)]
        peers += [dev(z, y, c, xp(o)) for o in range(1, nx)]
        bar = pltpu.get_barrier_semaphore()
        for to in peers:
            pl.semaphore_signal(bar, inc=1, device_id=to, device_id_type=pl.DeviceIdType.MESH)
        pl.semaphore_wait(bar, len(peers))

    def first_sends():
        for j in range(2):
            for i, w_ref in enumerate((wq_ref, wk_ref, wv_ref)):
                to = ws[j].at[rows(2 * chip + c, wrows), i * HDIM:(i + 1) * HDIM]
                sent([rcopy(w_ref.at[:, rows(2 * (1 - c) + j, HDIM)], to, w_s.at[j], w_r.at[j], mate)])
            ref = ws[j].at[rows(2 * chip + 1 - c, wrows)]
            left(ref, w_s.at[j])
            expect(("w", j), landing(ref, w_r.at[j]))
        z_step("az", a_ref, za, az_s, az_r)
        local.pop()()
        gains[x] = gain_low[...].astype(F32).reshape(1, width)
        sent(rcopy(gains.at[x], gains.at[x], gn_s, gn_r, dev(z, y, c, xp(o))) for o in far(nx))
        left(gains.at[pl.ds(0, nx - 1)], gn_s)
        expect("gains", landing(gains.at[pl.ds(0, nx - 1)], gn_r))

    def weights_own():
        for wait in local:
            wait()
        for j in range(2):
            arrived(("w", j))
            left(ws[j].at[pl.ds(0, (ny - 1) * crows)], p1_s.at[j, 0])
            count = sum(goes(d, age, k) for d in range(2) for age in range(last + 1) for k in range(subs))
            left(ws[j].at[pl.ds(0, count * crows)], p2_s.at[j, 0, 0, 0])
        for d in range(2):
            if goes(d, 0, 0):
                for j in range(2):
                    sent([p2(j, d, 0, 0)])
        for o in order:
            for j in range(2):
                sent([p1(j, o)])
        expect("p1", *(functools.partial(p1_wait, j, k) for k in order for j in range(2)))

    def act_y():
        arrived("az")
        sa[...] = swapped(za[...], nz, ny)
        y_step("ay", sa, xf, c * tokens, own_cols, ay_s.at[0], ay_r, True)
        xf[pl.ds(pl.multiple_of(c * tokens + y * yrows, yrows), yrows), own_cols] = sa[rows(y, yrows), :]

    def weights_0(ks):
        arriving.pop("p1", None)
        for k in ks:
            for j in range(2):
                p1_wait(j, k)
                for d in range(2):
                    if goes(d, 0, k):
                        sent([p2(j, d, 0, k)])

    def ac(at):
        ref = xf.at[own_rows, rows(at, width)]
        sent([rcopy(ref, ref, ac_s, ac_r, mate)])

    def act_x():
        def piece(at, cols):
            return xf.at[pl.ds(pl.multiple_of(c * tokens + at * yrows, yrows), yrows), cols]

        for oy in [0] + order:
            at = yp(oy)
            ref = piece(at, own_cols)
            if oy:
                landing(ref, ay_r.at[at])()
            sent(rcopy(ref, ref, ax_s.at[0], ax_r.at[x], dev(z, y, c, xp(o))) for o in far(nx))
        ac(x)
        for o in range(1, nx):
            ref = xf.at[own_rows, rows(xp(o), width)]
            expect(("ax", o), landing(ref, ax_r.at[xp(o)]))
            left(ref, ax_s.at[0])

    def grad_z():
        z_step("oz", og_ref, zg, oz_s.at[0], oz_r.at[0])

    def grad_y():
        arrived("oz")
        sg[0] = swapped(zg[...], nz, ny)
        y_step("oy", sg.at[0], sg.at[1], 0, all_cols, oy_s.at[0], oy_r.at[0])
        sg[1, rows(y, yrows), :] = sg[0, rows(y, yrows), :]

    def act_c():
        for o in reversed(far(nx)):
            arrived(("ax", o))
            ac(xp(o))

    def grad_c():
        arrived("oy")
        sent([rcopy(sg.at[1, :, rows(1 - c, 2 * HDIM)], ogf.at[own_rows], oc_s, oc_r, mate)])
        left(ogf.at[own_rows], oc_s)
        expect("oc", landing(ogf.at[mate_rows], oc_r))
        ogf[own_rows, :] = sg[1, :, rows(c, 2 * HDIM)]

    def norm():
        left(xf.at[own_rows], ac_s)
        landing(xf.at[mate_rows], ac_r)()
        arrived("gains")
        square_sum = jnp.zeros((2 * tokens, 1), F32)
        for at in range(nx):
            act = xf[:, at * width:(at + 1) * width].astype(F32)
            square_sum += jnp.sum(act * act, axis=1, keepdims=True)
        inverse_rms = lax.rsqrt(square_sum / model + EPS)
        for at in range(nx):
            act = xf[:, at * width:(at + 1) * width].astype(F32)
            nrm[:, at * width:(at + 1) * width] = (act * inverse_rms * gains[at]).astype(BF16)
        state["inverse_rms"] = inverse_rms

    def grad_wait():
        arrived("oc")

    def attention(h):
        i = lax.broadcasted_iota(jnp.int32, (2 * tokens, 1), 0)
        j = lax.broadcasted_iota(jnp.int32, (1, 2 * tokens), 1)

        def frame_of(r):
            core = lax.div(r, tokens)
            yy = lax.rem(lax.div(r, yrows), ny)
            zz = lax.rem(lax.div(r, 2), nz)
            return (zz * ny + yy) * 2 + core

        causal = (frame_of(i) >= frame_of(j)) & (lax.rem(i, 2) == lax.rem(j, 2))
        scale = HDIM ** (-0.5)
        proj = dot(nrm[...], ws[h][...])
        low = proj.astype(BF16)
        q, k, v = low[:, :HDIM], low[:, HDIM:2 * HDIM], low[:, 2 * HDIM:]
        g = ogf[:, h * HDIM:(h + 1) * HDIM]
        scores = dot(q, k, NT) * scale
        exps = jnp.where(causal, jnp.exp(jnp.where(causal, scores, 0.0)), 0.0)
        probs = exps / jnp.sum(exps, axis=1, keepdims=True)
        dprobs = dot(g, v, NT)
        delta = jnp.sum(probs * dprobs, axis=1, keepdims=True)
        dscores = (probs * (dprobs - delta) * scale).astype(BF16)
        gq = dot(dscores, k).astype(BF16)
        gk = dot(dscores, q, TN).astype(BF16)
        gv = dot(probs.astype(BF16), g, TN).astype(BF16)
        inner = state.get("inner", 0.0)
        for n, part_of in enumerate((gq, gk, gv)):
            gmix[h, :, n * HDIM:(n + 1) * HDIM] = part_of
            inner += jnp.sum(part_of.astype(F32) * proj[:, n * HDIM:(n + 1) * HDIM], axis=1, keepdims=True)
        state["inner"] = inner

    xorder = tuple(far(nx)) + (0,)

    def combine(b):
        arrived(("pr", b))
        o = xorder[b]
        total = ig[b, own_rows, :] + part[b]
        if b < nx - 1:
            xsend[b] = total.astype(BF16)
            sent([rcopy(xsend.at[b], xrecv.at[b], xs_s.at[b], xs_r.at[b], dev(z, y, c, xp(o)))])
            left(xsend.at[b], xs_s.at[b])
            expect(("xs", b), landing(xrecv.at[b], xs_r.at[b]))
        else:
            ig[b, own_rows, :] = total
        arrived(("gp", b))
        gsend[b] = gsum[b] + gpart[b]
        if b < nx - 1:
            sent([rcopy(gsend.at[b], gx.at[b], gx_s.at[b], gx_r.at[b], dev(z, y, c, xp(o)))])
            left(gsend.at[b], gx_s.at[b])
            expect(("gx", b), landing(gx.at[b], gx_r.at[b]))
        else:
            gx[b] = gsend[b]

    def backward():
        inner = state["inner"] / model
        inverse_rms = state["inverse_rms"]
        for b, o in enumerate(xorder):
            at = xp(o)
            feats = rows(at, width)
            gn = dot(gmix[0], w0[feats, :], NT) + dot(gmix[1], w1[feats, :], NT)
            act = xf[:, feats].astype(F32) * inverse_rms
            gsum[b] = jnp.sum(gn * act, axis=0, keepdims=True)
            ig[b] = inverse_rms * (gn * gains[at] - act * inner)
            sent([rcopy(ig.at[b, mate_rows], part.at[b], pr_s.at[b], pr_r.at[b], mate)])
            left(part.at[b], pr_s.at[b])
            expect(("pr", b), landing(part.at[b], pr_r.at[b]))
            sent([rcopy(gsum.at[b], gpart.at[b], gp_s.at[b], gp_r.at[b], mate)])
            left(gsum.at[b], gp_s.at[b])
            expect(("gp", b), landing(gpart.at[b], gp_r.at[b]))
            if b > 0:
                combine(b - 1)
        combine(nx - 1)

    def back_y():
        drain()
        total = ig[nx - 1, own_rows, :]
        for b in range(nx - 1):
            arrived(("xs", b))
            total += xrecv[b].astype(F32)
        ysend[...] = total.astype(BF16)
        y_step("by", ysend, yrecv, 0, all_cols, oy_s.at[1], oy_r.at[1])
        yrecv[rows(y, yrows), :] = ysend[rows(y, yrows), :]
        for b in range(nx - 1):
            arrived(("gx", b))
        gy[y] = jnp.sum(gx[...], axis=0)
        sent(rcopy(gy.at[y], gy.at[y], gy_s, gy_r, dev(z, yp(o), c, x)) for o in far(ny))
        left(gy.at[pl.ds(0, ny - 1)], gy_s)
        expect("gy", landing(gy.at[pl.ds(0, ny - 1)], gy_r))

    def back_z():
        arrived("by")
        zsend[...] = swapped(yrecv[...], ny, nz)
        z_step("bz", zsend, zrecv, oz_s.at[1], oz_r.at[1])
        zrecv[rows(z, zrows), :] = zsend[rows(z, zrows), :]
        arrived("gy")
        gz[z] = jnp.sum(gy[...], axis=0)
        sent(rcopy(gz.at[z], gz.at[z], gz_s, gz_r, dev(zp(o), y, c, x)) for o in far(nz))
        left(gz.at[pl.ds(0, nz - 1)], gz_s)
        expect("gz", landing(gz.at[pl.ds(0, nz - 1)], gz_r))

    def finish():
        drain()
        arrived("bz")
        out_ref[...] = zrecv[...]
        arrived("gz")
        gg_ref[...] = jnp.sum(gz[...], axis=0).reshape(width)

    step = functools.partial
    stages = [
        begin, first_sends, weights_own, step(weights_0, order[:4]), act_y, step(weights_0, order[4:]),
        grad_z, step(hop, 1), step(hop, 2, (0,)), act_x, step(hop, 2, (1,)), grad_y,
        step(hop, 3, (0,)), act_c, step(hop, 3, (1,)), norm, grad_c, step(hop, 4), grad_wait,
        step(attention, 0), step(attention, 1),
        backward, back_y, back_z, finish,
    ]
    for stage in stages:
        stage()
    drain()


def shards(nz, ny, nx, activations, norm_gain, w_query, w_key, w_value, out_grad):
    tokens, width = activations.shape
    model = width * nx
    wcols = 3 * HDIM
    wrows = w_query.shape[0]
    vmem = pl.BlockSpec(memory_space=pltpu.VMEM)
    hbm = pl.BlockSpec(memory_space=pltpu.HBM)
    dma = pltpu.SemaphoreType.DMA
    ring = nz // 2
    scratch = [
        pltpu.VMEM((model, wcols), BF16),
        pltpu.VMEM((model, wcols), BF16),
        pltpu.VMEM((tokens, width), BF16),
        pltpu.VMEM((tokens, width), BF16),
        pltpu.VMEM((tokens, width), BF16),
        pltpu.VMEM((2, tokens, width), BF16),
        pltpu.VMEM((2 * tokens, model), BF16),
        pltpu.VMEM((2 * tokens, model), BF16),
        pltpu.VMEM((2 * tokens, 2 * HDIM), BF16),
        pltpu.VMEM((2, 2 * tokens, wcols), BF16),
        pltpu.VMEM((nx, 1, width), F32),
        pltpu.VMEM((nx, 1, width), F32),
        pltpu.VMEM((nx, 1, width), F32),
        pltpu.VMEM((nx, 1, width), F32),
        pltpu.VMEM((ny, 1, width), F32),
        pltpu.VMEM((nz, 1, width), F32),
        pltpu.VMEM((nx, 1, width), F32),
        pltpu.VMEM((nx, 2 * tokens, width), F32),
        pltpu.VMEM((nx, tokens, width), F32),
        pltpu.VMEM((nx, tokens, width), BF16),
        pltpu.VMEM((nx, tokens, width), BF16),
        pltpu.VMEM((tokens, width), BF16),
        pltpu.VMEM((tokens, width), BF16),
        pltpu.VMEM((tokens, width), BF16),
        pltpu.VMEM((tokens, width), BF16),
    ]
    scratch += [pltpu.VMEM((width,), BF16), dma((9,))]
    for shape in (
        (2,), (2, ny), (2, 2, ring, ny), (), (ny,), (nx,), (),
        (), (), (nx,), (nx,), (nx,), (nx,), (), (),
        (2,), (2,),
    ):
        scratch += [dma(shape), dma(shape)] if shape else [dma, dma]
    args = (activations, norm_gain, w_query, w_key, w_value, out_grad)
    args = tuple(pltpu.with_memory_space_constraint(arg, pltpu.HBM) for arg in args)
    return pl.pallas_call(
        functools.partial(kernel, nz, ny, nx),
        out_shape=(
            jax.ShapeDtypeStruct((tokens, width), BF16),
            jax.ShapeDtypeStruct((width,), F32),
        ),
        in_specs=[hbm] * 6,
        out_specs=(vmem, vmem),
        scratch_shapes=scratch,
        compiler_params=pltpu.CompilerParams(
            collective_id=0, has_side_effects=True, vmem_limit_bytes=24 * 1024 * 1024
        ),
    )(*args)


def solution(mesh, nz=8, ny=8):
    nx = mesh.shape["heads"]
    in_specs = (
        P("frames", "heads"),
        P("heads"),
        P("frames", "heads"),
        P("frames", "heads"),
        P("frames", "heads"),
        P("frames", "heads"),
    )
    out_specs = (P("frames", "heads"), P("heads"))
    return jax.shard_map(
        functools.partial(shards, nz, ny, nx),
        mesh=mesh, in_specs=in_specs, out_specs=out_specs, check_vma=False,
    )
```

time: 684 us -> 74.7 us (0.11)
  waiting for transfers between devices: 293 us -> 0 us
  blocking collectives: 278 us -> 0 us
  Pallas kernels: 0 us -> 72.7 us
  starting transfers between devices: 55.8 us -> 0 us
  local copies, waits for them, and re-layouts: 20.1 us -> 1.24 us
  between operations: 14.1 us -> 0.64 us
  other arithmetic: 11 us -> 0 us
  matrix products: 10.6 us -> 0 us
    psum x3 -> x0, blocking collectives: 268 us -> none  [the longest x1 252 us: shards(): lax.psum(jnp.sum(grad_normed * values_f * inverse_rms, axis=0), 'frames')]
    all_gather x3 -> x0, waiting for transfers between devices: 207 us -> none  [the longest x1 79.9 us: shards(): lax.all_gather(w_key, 'frames', axis=0, tiled=True)]
    pallas_call x0 -> x1, Pallas kernels: none -> 72.7 us  [shards(): pl.pallas_call(functools.partial(kernel, nz, ny, nx), out_shape=(jax.Shap...]
    all_to_all x7 -> x0, waiting for transfers between devices: 65 us -> none  [the longest x1 12.5 us: shards(): lax.all_to_all(dquery, 'frames', split_axis=0, concat_axis=1, tiled=True)]
    all_to_all x7 -> x0, starting transfers between devices: 55.6 us -> none  [the longest x1 18.4 us: shards(): lax.all_to_all(layout[3], 'frames', split_axis=1, concat_axis=0, tiled=True)]
    reduce_scatter x1 -> x0, waiting for transfers between devices: 19.2 us -> none  [shards(): lax.psum_scatter(lax.dot_general(stacked, grad_mixed, (((1,), (1,)), ((),...]
    unnamed x25 -> x2, local copies, waits for them, and re-layouts: 14.5 us -> 1.24 us
    dot_general x7 -> x0, matrix products: 10.6 us -> none  [the longest x1 5.58 us: shards(): lax.dot_general(stacked, grad_mixed, (((1,), (1,)), ((), ())), preferred_...]
  transfers between devices with their start and end apart: 11 -> 0, of which waited for: 10 -> 0; matrix products, arithmetic and copies ran while one was open for 5% -> 0% of each run, Pallas kernels for 0% -> 0%
where the time goes in v2:
time: 74.7 us; the launch traced here: 74.5 us
  Pallas kernels  72.7 us (97%)
  local copies, waits for them, and re-layouts  1.24 us (2%)
    pallas_call x1, Pallas kernels, shards(): pl.pallas_call(functools.partial(kernel, nz, ny, nx), out_shape=(jax.Shap...  72.7 us

profile of v2, /device:TPU:1, one launch (start us, length us, event | category | flops | bytes accessed | tf_op | source)
XLA Modules:
  0.0 74.5 jit_solution(1770083224312154557)
XLA Ops:
  0.6 72.7 %shard_map.77 = (bf16[128,512]{1,0:T(8,128)(2,1)S(1)}, f32[512]{0:T(512)S(1)}) custom-call(bf16[128,512]{1,0:T(8,128)(2,1)} %a_ref.1, bf16[512]{0:T(512)(128)(2,1)} %gain_ref.1, bf16[16,512]{1,0:T(8,128)(2,1)} %wq_ref.1, bf16[16,512]{1,0:T(8,128)(2,1)} %wk_ref.1, bf16[16,512]{1,0:T(8,128)(2,1)} %wv_ref.1, bf16[128,512]{1,0:T(8,128)(2,1)} %og_ref.1), custom_call_target="tpu_custom_call" | custom-call | tf_op jit(solution)/shard_map/pallas_call | solution.py:481
  73.3 0.7 copy.10
  74.0 0.6 copy.11

commit v3 on v2

--- a/solution.py
+++ b/solution.py
@@ -25,7 +25,7 @@
     out_ref, gg_ref,
     w0, w1, za, zg, sa, sg, xf, nrm, ogf, gmix,
     gains, gsum, gpart, gx, gy, gz, gsend, ig, part, xsend, xrecv, ysend, yrecv, zsend, zrecv,
-    gain_low, l_s, w_s, w_r, p1_s, p1_r, p2_s, p2_r, az_s, az_r, ay_s, ay_r, ax_s, ax_r, ac_s, ac_r,
+    gain_low, hot, l_s, w_s, w_r, p1_s, p1_r, p2_s, p2_r, az_s, az_r, ay_s, ay_r, ax_s, ax_r, ac_s, ac_r,
     oc_s, oc_r, gn_s, gn_r, pr_s, pr_r, xs_s, xs_r, gp_s, gp_r, gx_s, gx_r, gy_s, gy_r, gz_s, gz_r,
     oy_s, oy_r, oz_s, oz_r,
 ):
@@ -121,13 +121,19 @@
         if not by_piece:
             expect(name, landing(bulk, r))
 
-    def swapped(value, na, nb):
-        i = lax.broadcasted_iota(jnp.int32, (tokens, tokens), 0)
-        j = lax.broadcasted_iota(jnp.int32, (tokens, tokens), 1)
-        b = lax.div(i, 2 * na)
-        a = lax.rem(lax.div(i, 2), na)
-        hot = jnp.where(j == (a * nb + b) * 2 + lax.rem(i, 2), 1.0, 0.0).astype(BF16)
-        return dot(hot, value).astype(BF16)
+    def swap_rows(back):
+        i = lax.broadcasted_iota(jnp.int32, (tokens, tokens), 1 if back else 0)
+        j = lax.broadcasted_iota(jnp.int32, (tokens, tokens), 0 if back else 1)
+        bits = nz.bit_length()
+        source = (i & (nz - 1)) * zrows + (i >> bits) * 2 + ((i >> (bits - 1)) & 1)
+        return jnp.where(j == source, 1.0, 0.0).astype(BF16)
+
+    def swapped(value, back=0):
+        return dot(hot[back], value).astype(BF16)
+
+    def of_position(value, p):
+        split = value.reshape(2 * ny, 2, nz, value.shape[1])
+        return split[:, p].reshape(tokens, value.shape[1])
 
     def p1(j, o):
         ref = ws[j].at[block(z, y)]
@@ -173,6 +179,12 @@
                 p2(j, d, age, k).start()
 
         each(act, halves)
+
+    def last_hop(j):
+        for k in range(subs):
+            for d in range(2):
+                if goes(d, last, k):
+                    landing(place(j, d, last + 1, k), p2_r.at[j, d, last, k])()
 
     order = sorted(range(1, ny), key=lambda o: min(o, ny - o))
 
@@ -198,6 +210,9 @@
         to_here(a_ref.at[rows(z, zrows)], za.at[rows(z, zrows)], 6)
         to_here(og_ref.at[rows(z, zrows)], zg.at[rows(z, zrows)], 7)
         to_here(gain_ref, gain_low, 8)
+
+        hot[0] = swap_rows(False)
+        hot[1] = swap_rows(True)
 
         peers = [mate]
         peers += [dev(z, yp(o), c, x) for o in range(1, ny)]
@@ -242,7 +257,7 @@
 
     def act_y():
         arrived("az")
-        sa[...] = swapped(za[...], nz, ny)
+        sa[...] = swapped(za[...])
         y_step("ay", sa, xf, c * tokens, own_cols, ay_s.at[0], ay_r, True)
         xf[pl.ds(pl.multiple_of(c * tokens + y * yrows, yrows), yrows), own_cols] = sa[rows(y, yrows), :]
 
@@ -280,7 +295,7 @@
 
     def grad_y():
         arrived("oz")
-        sg[0] = swapped(zg[...], nz, ny)
+        sg[0] = swapped(zg[...])
         y_step("oy", sg.at[0], sg.at[1], 0, all_cols, oy_s.at[0], oy_r.at[0])
         sg[1, rows(y, yrows), :] = sg[0, rows(y, yrows), :]
 
@@ -313,98 +328,115 @@
     def grad_wait():
         arrived("oc")
 
-    def attention(h):
-        i = lax.broadcasted_iota(jnp.int32, (2 * tokens, 1), 0)
-        j = lax.broadcasted_iota(jnp.int32, (1, 2 * tokens), 1)
+    def project(h):
+        proj = dot(nrm[...], ws[h][...])
+        for p in range(2):
+            state["proj", p, h] = of_position(proj, p)
+
+    def attention(p):
+        i = lax.broadcasted_iota(jnp.int32, (tokens, 1), 0)
+        j = lax.broadcasted_iota(jnp.int32, (1, tokens), 1)
 
         def frame_of(r):
-            core = lax.div(r, tokens)
-            yy = lax.rem(lax.div(r, yrows), ny)
-            zz = lax.rem(lax.div(r, 2), nz)
-            return (zz * ny + yy) * 2 + core
-
-        causal = (frame_of(i) >= frame_of(j)) & (lax.rem(i, 2) == lax.rem(j, 2))
+            return ((r & (nz - 1)) * ny + (lax.div(r, nz) & (ny - 1))) * 2 + lax.div(r, nz * ny)
+
+        causal = frame_of(i) >= frame_of(j)
         scale = HDIM ** (-0.5)
-        proj = dot(nrm[...], ws[h][...])
-        low = proj.astype(BF16)
-        q, k, v = low[:, :HDIM], low[:, HDIM:2 * HDIM], low[:, 2 * HDIM:]
-        g = ogf[:, h * HDIM:(h + 1) * HDIM]
-        scores = dot(q, k, NT) * scale
-        exps = jnp.where(causal, jnp.exp(jnp.where(causal, scores, 0.0)), 0.0)
-        probs = exps / jnp.sum(exps, axis=1, keepdims=True)
-        dprobs = dot(g, v, NT)
-        delta = jnp.sum(probs * dprobs, axis=1, keepdims=True)
-        dscores = (probs * (dprobs - delta) * scale).astype(BF16)
-        gq = dot(dscores, k).astype(BF16)
-        gk = dot(dscores, q, TN).astype(BF16)
-        gv = dot(probs.astype(BF16), g, TN).astype(BF16)
-        inner = state.get("inner", 0.0)
-        for n, part_of in enumerate((gq, gk, gv)):
-            gmix[h, :, n * HDIM:(n + 1) * HDIM] = part_of
-            inner += jnp.sum(part_of.astype(F32) * proj[:, n * HDIM:(n + 1) * HDIM], axis=1, keepdims=True)
-        state["inner"] = inner
+        inner = jnp.zeros((tokens, 1), F32)
+        for h in range(2):
+            proj = state["proj", p, h]
+            low = proj.astype(BF16)
+            q, k, v = low[:, :HDIM], low[:, HDIM:2 * HDIM], low[:, 2 * HDIM:]
+            g = of_position(ogf[:, h * HDIM:(h + 1) * HDIM].astype(F32), p).astype(BF16)
+            scores = dot(q, k, NT) * scale
+            exps = jnp.where(causal, jnp.exp(jnp.where(causal, scores, 0.0)), 0.0)
+            probs = exps / jnp.sum(exps, axis=1, keepdims=True)
+            dprobs = dot(g, v, NT)
+            delta = jnp.sum(probs * dprobs, axis=1, keepdims=True)
+            dscores = (probs * (dprobs - delta) * scale).astype(BF16)
+            gq = dot(dscores, k).astype(BF16)
+            gk = dot(dscores, q, TN).astype(BF16)
+            gv = dot(probs.astype(BF16), g, TN).astype(BF16)
+            for n, part_of in enumerate((gq, gk, gv)):
+                gmix[p, h, :, n * HDIM:(n + 1) * HDIM] = part_of
+                inner += jnp.sum(part_of.astype(F32) * proj[:, n * HDIM:(n + 1) * HDIM], axis=1, keepdims=True)
+        state["inner", p] = inner / model
 
     xorder = tuple(far(nx)) + (0,)
-
-    def combine(b):
-        arrived(("pr", b))
+    half = tokens // 2
+
+    def combine(p, b):
+        arrived(("pr", p, b))
         o = xorder[b]
-        total = ig[b, own_rows, :] + part[b]
+        total = ig[p, b, rows(c, half), :] + part[p, b]
         if b < nx - 1:
-            xsend[b] = total.astype(BF16)
-            sent([rcopy(xsend.at[b], xrecv.at[b], xs_s.at[b], xs_r.at[b], dev(z, y, c, xp(o)))])
-            left(xsend.at[b], xs_s.at[b])
-            expect(("xs", b), landing(xrecv.at[b], xs_r.at[b]))
+            xsend[p, b] = total.astype(BF16)
+            sems = xs_s.at[p, b], xs_r.at[p, b]
+            sent([rcopy(xsend.at[p, b], xrecv.at[p, b], *sems, dev(z, y, c, xp(o)))])
+            left(xsend.at[p, b], sems[0])
+            expect(("xs", p, b), landing(xrecv.at[p, b], sems[1]))
         else:
-            ig[b, own_rows, :] = total
-        arrived(("gp", b))
-        gsend[b] = gsum[b] + gpart[b]
-        if b < nx - 1:
-            sent([rcopy(gsend.at[b], gx.at[b], gx_s.at[b], gx_r.at[b], dev(z, y, c, xp(o)))])
-            left(gsend.at[b], gx_s.at[b])
-            expect(("gx", b), landing(gx.at[b], gx_r.at[b]))
-        else:
-            gx[b] = gsend[b]
-
-    def backward():
-        inner = state["inner"] / model
-        inverse_rms = state["inverse_rms"]
+            ig[p, b, rows(c, half), :] = total
+
+    def backward(p):
+        inner = state["inner", p]
+        inverse_rms = of_position(state["inverse_rms"], p)
         for b, o in enumerate(xorder):
             at = xp(o)
             feats = rows(at, width)
-            gn = dot(gmix[0], w0[feats, :], NT) + dot(gmix[1], w1[feats, :], NT)
-            act = xf[:, feats].astype(F32) * inverse_rms
-            gsum[b] = jnp.sum(gn * act, axis=0, keepdims=True)
-            ig[b] = inverse_rms * (gn * gains[at] - act * inner)
-            sent([rcopy(ig.at[b, mate_rows], part.at[b], pr_s.at[b], pr_r.at[b], mate)])
-            left(part.at[b], pr_s.at[b])
-            expect(("pr", b), landing(part.at[b], pr_r.at[b]))
-            sent([rcopy(gsum.at[b], gpart.at[b], gp_s.at[b], gp_r.at[b], mate)])
-            left(gsum.at[b], gp_s.at[b])
-            expect(("gp", b), landing(gpart.at[b], gp_r.at[b]))
-            if b > 0:
-                combine(b - 1)
-        combine(nx - 1)
+            gn = dot(gmix[p, 0], w0[feats, :], NT) + dot(gmix[p, 1], w1[feats, :], NT)
+            act = of_position(xf[:, feats].astype(F32), p) * inverse_rms
+            terms = jnp.sum(gn * act, axis=0, keepdims=True)
+            gsum[b] = gsum[b] + terms if p else terms
+            ig[p, b] = inverse_rms * (gn * gains[at] - act * inner)
+            sems = pr_s.at[p, b], pr_r.at[p, b]
+            sent([rcopy(ig.at[p, b, rows(1 - c, half)], part.at[p, b], *sems, mate)])
+            left(part.at[p, b], sems[0])
+            expect(("pr", p, b), landing(part.at[p, b], sems[1]))
+            if p and b > 0:
+                combine(p, b - 1)
+
+    def combine_first():
+        for b in range(nx):
+            combine(0, b)
+
+    def combine_last():
+        sent([rcopy(gsum, gpart, gp_s.at[0], gp_r.at[0], mate)])
+        early, leaving[:] = leaving[:], []
+        left(gsum, gp_s.at[0])
+        combine(1, nx - 1)
+        landing(gpart, gp_r.at[0])()
+        gsend[...] = gsum[...] + gpart[...]
+        gx[nx - 1] = gsend[nx - 1]
+        sent(
+            rcopy(gsend.at[b], gx.at[b], gx_s.at[0], gx_r.at[0], dev(z, y, c, xp(xorder[b]))) for b in range(nx - 1)
+        )
+        left(gsend.at[pl.ds(0, nx - 1)], gx_s.at[0])
+        expect("gx", landing(gx.at[pl.ds(0, nx - 1)], gx_r.at[0]))
+        for wait in early:
+            wait()
 
     def back_y():
-        drain()
-        total = ig[nx - 1, own_rows, :]
-        for b in range(nx - 1):
-            arrived(("xs", b))
-            total += xrecv[b].astype(F32)
-        ysend[...] = total.astype(BF16)
+        totals = []
+        for p in range(2):
+            total = ig[p, nx - 1, rows(c, half), :]
+            for b in range(nx - 1):
+                arrived(("xs", p, b))
+                total += xrecv[p, b].astype(F32)
+            totals.append(total.reshape(ny, 1, nz, width))
+        ysend[...] = jnp.concatenate(totals, axis=1).reshape(tokens, width).astype(BF16)
         y_step("by", ysend, yrecv, 0, all_cols, oy_s.at[1], oy_r.at[1])
         yrecv[rows(y, yrows), :] = ysend[rows(y, yrows), :]
-        for b in range(nx - 1):
-            arrived(("gx", b))
+        arrived("gx")
         gy[y] = jnp.sum(gx[...], axis=0)
         sent(rcopy(gy.at[y], gy.at[y], gy_s, gy_r, dev(z, yp(o), c, x)) for o in far(ny))
         left(gy.at[pl.ds(0, ny - 1)], gy_s)
         expect("gy", landing(gy.at[pl.ds(0, ny - 1)], gy_r))
+        drain()
 
     def back_z():
         arrived("by")
-        zsend[...] = swapped(yrecv[...], ny, nz)
+        zsend[...] = swapped(yrecv[...], 1)
         z_step("bz", zsend, zrecv, oz_s.at[1], oz_r.at[1])
         zrecv[rows(z, zrows), :] = zsend[rows(z, zrows), :]
         arrived("gy")
@@ -414,7 +446,6 @@
         expect("gz", landing(gz.at[pl.ds(0, nz - 1)], gz_r))
 
     def finish():
-        drain()
         arrived("bz")
         out_ref[...] = zrecv[...]
         arrived("gz")
@@ -422,11 +453,11 @@
 
     step = functools.partial
     stages = [
-        begin, first_sends, weights_own, step(weights_0, order[:4]), act_y, step(weights_0, order[4:]),
-        grad_z, step(hop, 1), step(hop, 2, (0,)), act_x, step(hop, 2, (1,)), grad_y,
-        step(hop, 3, (0,)), act_c, step(hop, 3, (1,)), norm, grad_c, step(hop, 4), grad_wait,
-        step(attention, 0), step(attention, 1),
-        backward, back_y, back_z, finish,
+        begin, first_sends, weights_own, step(weights_0, order), act_y, step(hop, 1), act_x, grad_z,
+        step(hop, 2), act_c, grad_y, step(hop, 3), grad_c, norm,
+        step(last_hop, 0), step(project, 0), step(last_hop, 1), step(project, 1), grad_wait,
+        step(attention, 0), step(backward, 0), combine_first, step(attention, 1), step(backward, 1), combine_last,
+        back_y, back_z, finish,
     ]
     for stage in stages:
         stage()
@@ -452,7 +483,7 @@
         pltpu.VMEM((2 * tokens, model), BF16),
         pltpu.VMEM((2 * tokens, model), BF16),
         pltpu.VMEM((2 * tokens, 2 * HDIM), BF16),
-        pltpu.VMEM((2, 2 * tokens, wcols), BF16),
+        pltpu.VMEM((2, 2, tokens, wcols), BF16),
         pltpu.VMEM((nx, 1, width), F32),
         pltpu.VMEM((nx, 1, width), F32),
         pltpu.VMEM((nx, 1, width), F32),
@@ -460,19 +491,19 @@
         pltpu.VMEM((ny, 1, width), F32),
         pltpu.VMEM((nz, 1, width), F32),
         pltpu.VMEM((nx, 1, width), F32),
-        pltpu.VMEM((nx, 2 * tokens, width), F32),
-        pltpu.VMEM((nx, tokens, width), F32),
-        pltpu.VMEM((nx, tokens, width), BF16),
-        pltpu.VMEM((nx, tokens, width), BF16),
+        pltpu.VMEM((2, nx, tokens, width), F32),
+        pltpu.VMEM((2, nx, tokens // 2, width), F32),
+        pltpu.VMEM((2, nx, tokens // 2, width), BF16),
+        pltpu.VMEM((2, nx, tokens // 2, width), BF16),
         pltpu.VMEM((tokens, width), BF16),
         pltpu.VMEM((tokens, width), BF16),
         pltpu.VMEM((tokens, width), BF16),
         pltpu.VMEM((tokens, width), BF16),
     ]
-    scratch += [pltpu.VMEM((width,), BF16), dma((9,))]
+    scratch += [pltpu.VMEM((width,), BF16), pltpu.VMEM((2, tokens, tokens), BF16), dma((9,))]
     for shape in (
         (2,), (2, ny), (2, 2, ring, ny), (), (ny,), (nx,), (),
-        (), (), (nx,), (nx,), (nx,), (nx,), (), (),
+        (), (), (2, nx), (2, nx), (nx,), (nx,), (), (),
         (2,), (2,),
     ):
         scratch += [dma(shape), dma(shape)] if shape else [dma, dma]

time: 74.7 us -> 73 us (0.977)
  the two profiles are of different devices: /device:TPU:1 before, /device:TPU:2 now
where the time goes in v3:
time: 73 us; the launch traced here: 72.9 us
  Pallas kernels  71 us (97%)
  local copies, waits for them, and re-layouts  1.24 us (2%)
    pallas_call x1, Pallas kernels, shards(): pl.pallas_call(functools.partial(kernel, nz, ny, nx), out_shape=(jax.Shap...  71 us

profile of v3, /device:TPU:2, one launch (start us, length us, event | category | flops | bytes accessed | tf_op | source)
XLA Modules:
  0.0 72.9 jit_solution(7518317050529898805)
XLA Ops:
  0.6 71.0 %shard_map.77 = (bf16[128,512]{1,0:T(8,128)(2,1)S(1)}, f32[512]{0:T(512)S(1)}) custom-call(bf16[128,512]{1,0:T(8,128)(2,1)} %a_ref.1, bf16[512]{0:T(512)(128)(2,1)} %gain_ref.1, bf16[16,512]{1,0:T(8,128)(2,1)} %wq_ref.1, bf16[16,512]{1,0:T(8,128)(2,1)} %wk_ref.1, bf16[16,512]{1,0:T(8,128)(2,1)} %wv_ref.1, bf16[128,512]{1,0:T(8,128)(2,1)} %og_ref.1), custom_call_target="tpu_custom_call" | custom-call | tf_op jit(solution)/shard_map/pallas_call | solution.py:512
  71.6 0.7 copy.10
  72.3 0.6 copy.11

commit v4 on v3

--- a/solution.py
+++ b/solution.py
@@ -200,6 +200,14 @@
             leaving.pop(0)()
 
     def begin():
+        peers = [mate]
+        peers += [dev(z, yp(o), c, x) for o in range(1, ny)]
+        peers += [dev(zp(o), y, c, x) for o in range(1, nz)]
+        peers += [dev(z, y, c, xp(o)) for o in range(1, nx)]
+        bar = pltpu.get_barrier_semaphore()
+        for to in peers:
+            pl.semaphore_signal(bar, inc=1, device_id=to, device_id_type=pl.DeviceIdType.MESH)
+
         for j in range(2):
             for i, w_ref in enumerate((wq_ref, wk_ref, wv_ref)):
                 to_here(
@@ -213,14 +221,6 @@
 
         hot[0] = swap_rows(False)
         hot[1] = swap_rows(True)
-
-        peers = [mate]
-        peers += [dev(z, yp(o), c, x) for o in range(1, ny)]
-        peers += [dev(zp(o), y, c, x) for o in range(1, nz)]
-        peers += [dev(z, y, c, xp(o)) for o in range(1, nx)]
-        bar = pltpu.get_barrier_semaphore()
-        for to in peers:
-            pl.semaphore_signal(bar, inc=1, device_id=to, device_id_type=pl.DeviceIdType.MESH)
         pl.semaphore_wait(bar, len(peers))
 
     def first_sends():
@@ -454,7 +454,7 @@
     step = functools.partial
     stages = [
         begin, first_sends, weights_own, step(weights_0, order), act_y, step(hop, 1), act_x, grad_z,
-        step(hop, 2), act_c, grad_y, step(hop, 3), grad_c, norm,
+        step(hop, 2), grad_y, step(hop, 3, (0,)), act_c, step(hop, 3, (1,)), grad_c, norm,
         step(last_hop, 0), step(project, 0), step(last_hop, 1), step(project, 1), grad_wait,
         step(attention, 0), step(backward, 0), combine_first, step(attention, 1), step(backward, 1), combine_last,
         back_y, back_z, finish,

time: 73 us -> 72.8 us (level)
  the two profiles are of different devices: /device:TPU:2 before, /device:TPU:1 now
where the time goes in v4:
time: 72.8 us; the launch traced here: 71.5 us
  Pallas kernels  69.7 us (96%)
  local copies, waits for them, and re-layouts  1.24 us (2%)
    pallas_call x1, Pallas kernels, shards(): pl.pallas_call(functools.partial(kernel, nz, ny, nx), out_shape=(jax.Shap...  69.7 us

profile of v4, /device:TPU:1, one launch (start us, length us, event | category | flops | bytes accessed | tf_op | source)
XLA Modules:
  0.0 71.5 jit_solution(16190968642608653917)
XLA Ops:
  0.6 69.7 %shard_map.77 = (bf16[128,512]{1,0:T(8,128)(2,1)S(1)}, f32[512]{0:T(512)S(1)}) custom-call(bf16[128,512]{1,0:T(8,128)(2,1)} %a_ref.1, bf16[512]{0:T(512)(128)(2,1)} %gain_ref.1, bf16[16,512]{1,0:T(8,128)(2,1)} %wq_ref.1, bf16[16,512]{1,0:T(8,128)(2,1)} %wk_ref.1, bf16[16,512]{1,0:T(8,128)(2,1)} %wv_ref.1, bf16[128,512]{1,0:T(8,128)(2,1)} %og_ref.1), custom_call_target="tpu_custom_call" | custom-call | tf_op jit(solution)/shard_map/pallas_call | solution.py:512
  70.3 0.7 copy.10
  71.0 0.6 copy.11

commit v5 on v4

--- a/solution.py
+++ b/solution.py
@@ -165,8 +165,7 @@
 
     def each(act, halves=(0, 1)):
         for half in halves:
-            @pl.loop(half * (subs // 2), (half + 1) * (subs // 2))
-            def _(k):
+            for k in range(half * (subs // 2), (half + 1) * (subs // 2)):
                 for j in range(2):
                     for d in range(2):
                         act(j, d, k, half * (subs - 1))

time: 72.8 us -> 72.8 us (level)
  no operation moved by 1% of the time
where the time goes in v5:
time: 72.8 us; the launch traced here: 71.5 us
  Pallas kernels  69.6 us (96%)
  local copies, waits for them, and re-layouts  1.24 us (2%)
    pallas_call x1, Pallas kernels, shards(): pl.pallas_call(functools.partial(kernel, nz, ny, nx), out_shape=(jax.Shap...  69.6 us

profile of v5, /device:TPU:1, one launch (start us, length us, event | category | flops | bytes accessed | tf_op | source)
XLA Modules:
  0.0 71.5 jit_solution(7311085157190508646)
XLA Ops:
  0.6 69.6 %shard_map.77 = (bf16[128,512]{1,0:T(8,128)(2,1)S(1)}, f32[512]{0:T(512)S(1)}) custom-call(bf16[128,512]{1,0:T(8,128)(2,1)} %a_ref.1, bf16[512]{0:T(512)(128)(2,1)} %gain_ref.1, bf16[16,512]{1,0:T(8,128)(2,1)} %wq_ref.1, bf16[16,512]{1,0:T(8,128)(2,1)} %wk_ref.1, bf16[16,512]{1,0:T(8,128)(2,1)} %wv_ref.1, bf16[128,512]{1,0:T(8,128)(2,1)} %og_ref.1), custom_call_target="tpu_custom_call" | custom-call | tf_op jit(solution)/shard_map/pallas_call | solution.py:511
  70.3 0.7 copy.10
  70.9 0.6 copy.11
